TPU v7x, 32 devices: a whole 2x2x4 slice. The times are simulated.
32 devices in a mesh: batch: 4 (over x, core), seq: 8 (over z, y).
Axes of the slice: x: 2, y: 2, z: 4, core: 2. Of those that a mesh axis runs over, the one named last changes fastest.
Arguments:
- tokens: bfloat16 [4, 8192, 768], P('batch', 'seq'), may hold values from -6 to 6
- glob_tokens: bfloat16 [4, 128, 768], P('batch'), may hold values from -6 to 6
- w_qkv: bfloat16 [768, 2304], replicated, may hold values from -0.21875 to 0.21875
- w_out: bfloat16 [768, 768], replicated, may hold values from -1.25 to 1.25
- w_up: bfloat16 [768, 3072], replicated, may hold values from -0.21875 to 0.21875
- w_down: bfloat16 [3072, 768], replicated, may hold values from -0.109375 to 0.109375
- vec_params: float32 [5, 768], replicated, may hold values from -1 to 2.5, as said below
- hidden_bias: float32 [3072], replicated, may hold values from -1.5 to 1.5
- row_qkv: float32 [768], P(('batch', 'seq')), may hold values from 2276.352 to 9105.408
- col_qkv: float32 [2304], replicated, may hold values from 2276.352 to 9105.408
- row_out: float32 [768], P(('batch', 'seq')), may hold values from 63.232 to 252.928
- col_out: float32 [768], replicated, may hold values from 63.232 to 252.928
- row_up: float32 [768], P(('batch', 'seq')), may hold values from 1896.96 to 7587.84
- col_up: float32 [3072], replicated, may hold values from 1896.96 to 7587.84
- row_down: float32 [3072], P(('batch', 'seq')), may hold values from 5058.56 to 20234.24
- col_down: float32 [768], replicated, may hold values from 5058.56 to 20234.24
- vec_state: float32 [5, 768], replicated, may hold values from 9484.8 to 37939.2
- bias_state: float32 [3072], replicated, may hold values from 1580.8 to 6323.2
- segments: int32 [4, 8192], P('batch'), may hold values from 0 to 3, as said below
- valid_mask: int32 [4, 8192], P('batch'), may hold values from 0 to 1
- out_cotangent: bfloat16 [4, 8192, 768], P('batch', 'seq'), may hold values from -6 to 6
- glob_cotangent: bfloat16 [4, 128, 768], P('batch'), may hold values from -6 to 6
Outputs:
- block_out: bfloat16 [4, 8192, 768], P('batch', 'seq')
- glob_out: bfloat16 [4, 128, 768], P('batch')
- tokens_grad: float32 [4, 8192, 768], P('batch', 'seq')
- glob_grad: float32 [4, 128, 768], P('batch')
- grad_qkv: float32 [768, 2304], P(('batch', 'seq'))
- row_qkv_new: float32 [768], P(('batch', 'seq'))
- col_qkv_new: float32 [2304], replicated
- new_qkv: float32 [768, 2304], P(('batch', 'seq'))
- grad_out: float32 [768, 768], P(('batch', 'seq'))
- row_out_new: float32 [768], P(('batch', 'seq'))
- col_out_new: float32 [768], replicated
- new_out: float32 [768, 768], P(('batch', 'seq'))
- grad_up: float32 [768, 3072], P(('batch', 'seq'))
- row_up_new: float32 [768], P(('batch', 'seq'))
- col_up_new: float32 [3072], replicated
- new_up: float32 [768, 3072], P(('batch', 'seq'))
- grad_down: float32 [3072, 768], P(('batch', 'seq'))
- row_down_new: float32 [3072], P(('batch', 'seq'))
- col_down_new: float32 [768], replicated
- new_down: float32 [3072, 768], P(('batch', 'seq'))
- vec_grad: float32 [5, 768], replicated
- vec_state_new: float32 [5, 768], replicated
- vec_new: float32 [5, 768], replicated
- bias_grad: float32 [3072], replicated
- bias_state_new: float32 [3072], replicated
- bias_new: float32 [3072], replicated
Inputs may be any that keep to these rules, and one draw needn't show every extreme that they name: `segments`: non-decreasing along each group. `vec_params`: rows 0 and 2 are positive.
All inputs are finite; a program needn't handle non-finite values.
Results may differ from a plain program's by a relative error of at most 0.013.
Values may be sent and summed in bfloat16 or wider, within the bound.
No kernel may reach another device: no remote copies, remote signals or barrier semaphores. Data moves between devices by JAX's collectives and lax.ppermute only.
A program may use at most 320 MiB of HBM per device.

v0:
```python
from functools import partial

import jax
import jax.numpy as jnp
from jax import lax
from jax.sharding import PartitionSpec as P

HEADS = 12
BLOCK = 512
STEP = 10


NEG_FILL = -1000000000.0
NORM_EPS = 1e-06
TINY_SQUARE = 1e-30
RATE_MATRIX = 0.03
RATE_VECTOR = 0.2


def with_halo(x, sides, width):
    for axis, dim in sides:
        size, length = (lax.axis_size(axis), x.shape[dim])
        up = [(i, (i + 1) % size) for i in range(size - 1)]
        down = [(j, i) for i, j in up]
        last = lax.slice_in_dim(x, length - width, length, axis=dim)
        initial = lax.slice_in_dim(x, 0, width, axis=dim)
        before = lax.ppermute(last, axis, up)
        after = lax.ppermute(initial, axis, down)
        x = jnp.concatenate([before, x, after], axis=dim)
    return x


def joined(part, axis, combine):
    gathered = jax.tree.map(lambda a: lax.all_gather(a, axis), part)

    def take(source):
        return jax.tree.map(lambda a: lax.dynamic_index_in_dim(a, source, 0, False), gathered)

    return lax.fori_loop(
        1, lax.axis_size(axis), lambda source, state: combine(state, take(source)), take(0)
    )


def from_behind(block, axis, distance):
    devices = range(lax.axis_size(axis))
    route = [(i - distance, i) for i in devices if i - distance in devices]
    return lax.ppermute(block, axis, route)


def layer_norm(values, norm_gain, norm_shift):
    average = jnp.mean(values, axis=-1, keepdims=True)
    centred = values - average
    variance = jnp.mean(centred * centred, axis=-1, keepdims=True)
    return centred * lax.rsqrt(variance + NORM_EPS) * norm_gain + norm_shift


def norm_terms(values, upstream):
    average = jnp.mean(values, axis=-1, keepdims=True)
    centred = values - average
    variance = jnp.mean(centred * centred, axis=-1, keepdims=True)
    normalized = centred * lax.rsqrt(variance + NORM_EPS)
    return (jnp.sum(upstream * normalized, axis=0), jnp.sum(upstream, axis=0))


def norm_backward(values, norm_gain, norm_shift, upstream):
    pullback = jax.vjp(lambda inner_rows: layer_norm(inner_rows, norm_gain, norm_shift), values)[1]
    return pullback(upstream)[0]


def dense(left_rows, right_rows):
    return jnp.dot(left_rows, right_rows, preferred_element_type=jnp.float32)


def dense_back(grad_rows, matrix):
    return lax.dot_general(
        grad_rows, matrix, (((1,), (1,)), ((), ())), preferred_element_type=jnp.float32
    )


def outer_sum(input_rows, grad_rows):
    return lax.dot_general(
        input_rows, grad_rows, (((0,), (0,)), ((), ())), preferred_element_type=jnp.float32
    )


def spread_blocks(values):
    grouped = values.reshape((-1, BLOCK) + values.shape[1:])
    return jnp.repeat(grouped, 2, axis=0)[1:-1]


def fold_blocks(values):
    zero_block = jnp.zeros((1,) + values.shape[1:], values.dtype)
    padded = jnp.concatenate([zero_block, values, zero_block], axis=0)
    paired = padded.reshape((-1, 2) + values.shape[1:])
    return jnp.sum(paired, axis=1).reshape((-1,) + values.shape[2:])


def combine_totals(earlier, later):
    top_score = jnp.maximum(earlier[0], later[0])
    return (
        top_score,
        earlier[1] * jnp.exp(earlier[0] - top_score) + later[1] * jnp.exp(later[0] - top_score),
    )


def body(
    tokens,
    glob_tokens,
    w_qkv,
    w_out,
    w_up,
    w_down,
    vec_params,
    hidden_bias,
    row_qkv,
    col_qkv,
    row_out,
    col_out,
    row_up,
    col_up,
    row_down,
    col_down,
    vec_state,
    bias_state,
    segments,
    valid_mask,
    out_cotangent,
    glob_cotangent,
):
    model_width = w_out.shape[0]
    head_size = model_width // HEADS
    score_scale = head_size ** (-0.5)
    half_rows = BLOCK // 2
    own_rows = tokens.shape[1]
    glob_count = glob_tokens.shape[1]
    halves = own_rows // half_rows
    seq_index = lax.axis_index("seq")
    row_start = seq_index * own_rows
    bf16 = jnp.bfloat16
    f32 = jnp.float32
    first_flag = seq_index == 0

    def counted(values):
        glob_rows = values[own_rows:] * first_flag.astype(values.dtype)
        return jnp.concatenate([values[:own_rows], glob_rows], axis=0)

    def to_heads(values):
        return values.reshape(values.shape[0], HEADS, head_size)

    rows_all = jnp.concatenate([tokens[0].astype(f32), glob_tokens[0].astype(f32)], axis=0)
    normed_low = layer_norm(rows_all, vec_params[0], vec_params[1]).astype(bf16)
    qkv_low = dense(normed_low, w_qkv).astype(bf16)
    pair_low = qkv_low[:own_rows, model_width:]
    query_own = to_heads(qkv_low[:own_rows, :model_width])
    key_own = to_heads(pair_low[:, :model_width])
    value_own = to_heads(pair_low[:, model_width:])
    glob_query = to_heads(qkv_low[own_rows:, :model_width])
    glob_key = to_heads(qkv_low[own_rows:, model_width : 2 * model_width])
    glob_value = to_heads(qkv_low[own_rows:, 2 * model_width :])
    extended = with_halo(pair_low, (("seq", 0),), half_rows)
    pair_blocks = spread_blocks(extended)
    key_blocks = pair_blocks[..., :model_width].reshape(halves, BLOCK, HEADS, head_size)
    value_blocks = pair_blocks[..., model_width:].reshape(halves, BLOCK, HEADS, head_size)
    seg_all = segments[0]
    mask_all = valid_mask[0]
    seg_ext = lax.dynamic_slice_in_dim(
        jnp.pad(seg_all, half_rows, constant_values=-1), row_start, own_rows + BLOCK
    )
    mask_ext = lax.dynamic_slice_in_dim(jnp.pad(mask_all, half_rows), row_start, own_rows + BLOCK)
    seg_own = lax.dynamic_slice_in_dim(seg_all, row_start, own_rows)
    mask_own = lax.dynamic_slice_in_dim(mask_all, row_start, own_rows) > 0
    seg_blocks = spread_blocks(seg_ext)
    mask_blocks = spread_blocks(mask_ext)
    allowed = (seg_own.reshape(halves, half_rows)[:, :, None] == seg_blocks[:, None, :]) & (
        mask_blocks[:, None, :] > 0
    )
    query_halves = query_own.reshape(halves, half_rows, HEADS, head_size)

    def local_scores():
        near_scores = (
            jnp.einsum("nqhe,nkhe->nhqk", query_halves, key_blocks, preferred_element_type=f32)
            * score_scale
        )
        near_scores = jnp.where(allowed[:, None], near_scores, NEG_FILL)
        far_scores = (
            jnp.einsum("nqhe,ghe->nhqg", query_halves, glob_key, preferred_element_type=f32)
            * score_scale
        )
        return jnp.concatenate([near_scores, far_scores], axis=-1)

    def glob_scores():
        to_tokens = (
            jnp.einsum("ghe,khe->hgk", glob_query, key_own, preferred_element_type=f32)
            * score_scale
        )
        to_tokens = jnp.where(mask_own[None, None, :], to_tokens, NEG_FILL)
        to_globs = (
            jnp.einsum("ghe,jhe->hgj", glob_query, glob_key, preferred_element_type=f32)
            * score_scale
        )
        return (to_tokens, to_globs)

    scores = local_scores()
    local_total = jax.nn.logsumexp(scores, axis=-1, keepdims=True)
    weights_low = jnp.exp(scores - local_total).astype(bf16)
    local_att = jnp.einsum(
        "nhqk,nkhe->nqhe", weights_low[..., :BLOCK], value_blocks, preferred_element_type=f32
    )
    local_att = local_att + jnp.einsum(
        "nhqg,ghe->nqhe", weights_low[..., BLOCK:], glob_value, preferred_element_type=f32
    )
    local_att = local_att.reshape(own_rows, model_width)
    to_tokens, to_globs = glob_scores()
    part_max = jnp.max(to_tokens, axis=-1)
    part_sum = jnp.sum(jnp.exp(to_tokens - part_max[..., None]), axis=-1)
    merged_max, merged_sum = joined((part_max, part_sum), "seq", combine_totals)
    top_score = jnp.maximum(merged_max, jnp.max(to_globs, axis=-1))
    glob_sum = merged_sum * jnp.exp(merged_max - top_score) + jnp.sum(
        jnp.exp(to_globs - top_score[..., None]), axis=-1
    )
    glob_total = (top_score + jnp.log(glob_sum))[..., None]
    token_weights_low = jnp.exp(to_tokens - glob_total).astype(bf16)
    self_weights_low = jnp.exp(to_globs - glob_total).astype(bf16)
    glob_part = jnp.einsum("hgk,khe->ghe", token_weights_low, value_own, preferred_element_type=f32)
    glob_att = lax.psum(glob_part, "seq")
    glob_att = glob_att + jnp.einsum(
        "hgj,jhe->ghe", self_weights_low, glob_value, preferred_element_type=f32
    )
    attended_low = jnp.concatenate(
        [local_att, glob_att.reshape(glob_count, model_width)], axis=0
    ).astype(bf16)
    mixed = rows_all + dense(attended_low, w_out)
    normed_two_low = layer_norm(mixed, vec_params[2], vec_params[3]).astype(bf16)
    hidden = dense(normed_two_low, w_up) + hidden_bias
    active_low = jax.nn.gelu(hidden, approximate=False).astype(bf16)
    result = mixed + (dense(active_low, w_down) + vec_params[4])
    upstream = jnp.concatenate(
        [out_cotangent[0].astype(f32), glob_cotangent[0].astype(f32)], axis=0
    )
    branch_low = upstream.astype(bf16)
    grad_down = outer_sum(counted(active_low), counted(branch_low))
    bias_two_grad = jnp.sum(counted(branch_low).astype(f32), axis=0)
    d_active = dense_back(branch_low, w_down)
    gelu_pull = jax.vjp(partial(jax.nn.gelu, approximate=False), hidden)[1]
    hidden_grad_low = gelu_pull(d_active)[0].astype(bf16)
    grad_up = outer_sum(counted(normed_two_low), counted(hidden_grad_low))
    bias_grad_part = jnp.sum(counted(hidden_grad_low).astype(f32), axis=0)
    d_normed_two = dense_back(hidden_grad_low, w_up)
    mixed_grad = upstream + norm_backward(mixed, vec_params[2], vec_params[3], d_normed_two)
    gain_two, shift_two = norm_terms(counted(mixed), counted(d_normed_two))
    attn_grad_low = mixed_grad.astype(bf16)
    grad_out = outer_sum(counted(attended_low), counted(attn_grad_low))
    heads_grad_low = dense_back(attn_grad_low, w_out).astype(bf16)
    local_grad = heads_grad_low[:own_rows].reshape(halves, half_rows, HEADS, head_size)
    glob_heads_grad = heads_grad_low[own_rows:].reshape(glob_count, HEADS, head_size)
    scores_again = local_scores()
    weights_again = jnp.exp(scores_again - local_total)
    weights_again_low = weights_again.astype(bf16)
    weight_grad = jnp.concatenate(
        [
            jnp.einsum("nqhe,nkhe->nhqk", local_grad, value_blocks, preferred_element_type=f32),
            jnp.einsum("nqhe,ghe->nhqg", local_grad, glob_value, preferred_element_type=f32),
        ],
        axis=-1,
    )
    row_inner = jnp.sum(weights_again * weight_grad, axis=-1, keepdims=True)
    score_grad_low = (weights_again * (weight_grad - row_inner)).astype(bf16)
    query_grad = jnp.einsum(
        "nhqk,nkhe->nqhe", score_grad_low[..., :BLOCK], key_blocks, preferred_element_type=f32
    )
    query_grad = (
        query_grad
        + jnp.einsum(
            "nhqg,ghe->nqhe", score_grad_low[..., BLOCK:], glob_key, preferred_element_type=f32
        )
    ) * score_scale
    key_block_grad = (
        jnp.einsum(
            "nhqk,nqhe->nkhe", score_grad_low[..., :BLOCK], query_halves, preferred_element_type=f32
        )
        * score_scale
    )
    value_block_grad = jnp.einsum(
        "nhqk,nqhe->nkhe", weights_again_low[..., :BLOCK], local_grad, preferred_element_type=f32
    )
    pair_grad_ext = fold_blocks(
        jnp.concatenate(
            [
                key_block_grad.reshape(halves, BLOCK, model_width),
                value_block_grad.reshape(halves, BLOCK, model_width),
            ],
            axis=-1,
        )
    )
    glob_key_part = (
        jnp.einsum(
            "nhqg,nqhe->ghe", score_grad_low[..., BLOCK:], query_halves, preferred_element_type=f32
        )
        * score_scale
    )
    glob_value_part = jnp.einsum(
        "nhqg,nqhe->ghe", weights_again_low[..., BLOCK:], local_grad, preferred_element_type=f32
    )
    glob_pair_part = jnp.concatenate(
        [
            glob_key_part.reshape(glob_count, model_width),
            glob_value_part.reshape(glob_count, model_width),
        ],
        axis=-1,
    )
    from_right = from_behind(pair_grad_ext[:half_rows].astype(jnp.bfloat16), "seq", -1).astype(
        jnp.float32
    )
    from_left = from_behind(
        pair_grad_ext[own_rows + half_rows :].astype(jnp.bfloat16), "seq", 1
    ).astype(jnp.float32)
    pair_grad = pair_grad_ext[half_rows : own_rows + half_rows]
    pair_grad = pair_grad.at[:half_rows].add(from_left).at[own_rows - half_rows :].add(from_right)
    tokens_again, globs_again = glob_scores()
    token_weights = jnp.exp(tokens_again - glob_total)
    self_weights = jnp.exp(globs_again - glob_total)
    token_weight_grad = jnp.einsum(
        "ghe,khe->hgk", glob_heads_grad, value_own, preferred_element_type=f32
    )
    self_weight_grad = jnp.einsum(
        "ghe,jhe->hgj", glob_heads_grad, glob_value, preferred_element_type=f32
    )
    part_inner = jnp.sum(token_weights * token_weight_grad, axis=-1)
    glob_inner = lax.psum(part_inner, "seq") + jnp.sum(self_weights * self_weight_grad, axis=-1)
    token_score_low = (token_weights * (token_weight_grad - glob_inner[..., None])).astype(bf16)
    self_score_low = (self_weights * (self_weight_grad - glob_inner[..., None])).astype(bf16)
    glob_query_part = (
        jnp.einsum("hgk,khe->ghe", token_score_low, key_own, preferred_element_type=f32)
        * score_scale
    )
    key_from_glob = (
        jnp.einsum("hgk,ghe->khe", token_score_low, glob_query, preferred_element_type=f32)
        * score_scale
    )
    value_from_glob = jnp.einsum(
        "hgk,ghe->khe", token_weights.astype(bf16), glob_heads_grad, preferred_element_type=f32
    )
    pair_grad = pair_grad + jnp.concatenate(
        [
            key_from_glob.reshape(own_rows, model_width),
            value_from_glob.reshape(own_rows, model_width),
        ],
        axis=-1,
    )
    query_sum, pair_sum = lax.psum(
        (glob_query_part.reshape(glob_count, model_width), glob_pair_part), "seq"
    )
    glob_query_grad = query_sum + (
        jnp.einsum("hgj,jhe->ghe", self_score_low, glob_key, preferred_element_type=f32)
        * score_scale
    ).reshape(glob_count, model_width)
    glob_key_grad = pair_sum[:, :model_width] + (
        jnp.einsum("hgj,ghe->jhe", self_score_low, glob_query, preferred_element_type=f32)
        * score_scale
    ).reshape(glob_count, model_width)
    glob_value_grad = pair_sum[:, model_width:] + jnp.einsum(
        "hgj,ghe->jhe", self_weights_low, glob_heads_grad, preferred_element_type=f32
    ).reshape(glob_count, model_width)
    qkv_grad_low = jnp.concatenate(
        [
            jnp.concatenate([query_grad.reshape(own_rows, model_width), pair_grad], axis=-1),
            jnp.concatenate([glob_query_grad, glob_key_grad, glob_value_grad], axis=-1),
        ],
        axis=0,
    ).astype(bf16)
    grad_qkv = outer_sum(counted(normed_low), counted(qkv_grad_low))
    d_normed = dense_back(qkv_grad_low, w_qkv)
    row_grad = mixed_grad + norm_backward(rows_all, vec_params[0], vec_params[1], d_normed)
    gain_one, shift_one = norm_terms(counted(rows_all), counted(d_normed))
    vec_grad_part = jnp.stack([gain_one, shift_one, gain_two, shift_two, bias_two_grad])
    shards = (
        lax.psum_scatter(grad_qkv, ("batch", "seq"), scatter_dimension=0, tiled=True),
        lax.psum_scatter(grad_out, ("batch", "seq"), scatter_dimension=0, tiled=True),
        lax.psum_scatter(grad_up, ("batch", "seq"), scatter_dimension=0, tiled=True),
        lax.psum_scatter(grad_down, ("batch", "seq"), scatter_dimension=0, tiled=True),
    )
    decay_rate = 1.0 - STEP ** (-0.8)
    owner_index = lax.axis_index(("batch", "seq"))
    matrices = (w_qkv, w_out, w_up, w_down)
    row_olds = (row_qkv, row_out, row_up, row_down)
    col_olds = (col_qkv, col_out, col_up, col_down)
    squares = [shard_grad * shard_grad + TINY_SQUARE for shard_grad in shards]
    row_news = [
        decay_rate * old_rows + (1.0 - decay_rate) * jnp.mean(square, axis=1)
        for old_rows, square in zip(row_olds, squares)
    ]
    col_parts = [jnp.sum(square, axis=0) for square in squares]
    row_totals = jnp.stack([jnp.sum(row_new) for row_new in row_news])
    stats = lax.psum(
        (
            col_parts[0],
            col_parts[1],
            col_parts[2],
            col_parts[3],
            row_totals,
            vec_grad_part,
            bias_grad_part,
        ),
        ("batch", "seq"),
    )
    updates = []
    for matrix_index in range(4):
        full_rows = matrices[matrix_index].shape[0]
        shard_rows = shards[matrix_index].shape[0]
        col_new = decay_rate * col_olds[matrix_index] + (1.0 - decay_rate) * (
            stats[matrix_index] / full_rows
        )
        row_mean = stats[4][matrix_index] / full_rows
        master = lax.dynamic_slice_in_dim(
            matrices[matrix_index], owner_index * shard_rows, shard_rows, 0
        ).astype(f32)
        estimate = row_news[matrix_index][:, None] * col_new[None, :] / row_mean
        new_weight = master - RATE_MATRIX * shards[matrix_index] * lax.rsqrt(estimate)
        updates += [shards[matrix_index], row_news[matrix_index], col_new, new_weight]
    vec_grad = stats[5]
    bias_grad = stats[6]
    vec_state_new = decay_rate * vec_state + (1.0 - decay_rate) * (
        vec_grad * vec_grad + TINY_SQUARE
    )
    vec_new = vec_params - RATE_VECTOR * vec_grad * lax.rsqrt(vec_state_new)
    bias_state_new = decay_rate * bias_state + (1.0 - decay_rate) * (
        bias_grad * bias_grad + TINY_SQUARE
    )
    bias_new = hidden_bias - RATE_VECTOR * bias_grad * lax.rsqrt(bias_state_new)
    return (
        result[:own_rows].astype(bf16)[None],
        result[own_rows:].astype(bf16)[None],
        row_grad[:own_rows][None],
        row_grad[own_rows:][None],
        updates[0],
        updates[1],
        updates[2],
        updates[3],
        updates[4],
        updates[5],
        updates[6],
        updates[7],
        updates[8],
        updates[9],
        updates[10],
        updates[11],
        updates[12],
        updates[13],
        updates[14],
        updates[15],
        vec_grad,
        vec_state_new,
        vec_new,
        bias_grad,
        bias_state_new,
        bias_new,
    )


def solution(mesh):
    in_specs = (
        P("batch", "seq", None),
        P("batch", None, None),
        P(),
        P(),
        P(),
        P(),
        P(),
        P(),
        P(("batch", "seq")),
        P(),
        P(("batch", "seq")),
        P(),
        P(("batch", "seq")),
        P(),
        P(("batch", "seq")),
        P(),
        P(),
        P(),
        P("batch", None),
        P("batch", None),
        P("batch", "seq", None),
        P("batch", None, None),
    )
    out_specs = (
        P("batch", "seq", None),
        P("batch", None, None),
        P("batch", "seq", None),
        P("batch", None, None),
        P(("batch", "seq"), None),
        P(("batch", "seq")),
        P(),
        P(("batch", "seq"), None),
        P(("batch", "seq"), None),
        P(("batch", "seq")),
        P(),
        P(("batch", "seq"), None),
        P(("batch", "seq"), None),
        P(("batch", "seq")),
        P(),
        P(("batch", "seq"), None),
        P(("batch", "seq"), None),
        P(("batch", "seq")),
        P(),
        P(("batch", "seq"), None),
        P(),
        P(),
        P(),
        P(),
        P(),
        P(),
    )
    return jax.shard_map(body, mesh=mesh, in_specs=in_specs, out_specs=out_specs, check_vma=False)
```

profile of v0, /device:TPU:0, one launch (start us, length us, event | category | flops | bytes accessed | tf_op | source)
XLA Modules:
  0.0 1270.5 jit_solution(12799338279582984635)
XLA Ops:
  60.4 32.0 %all-gather.3 = f32[8,12,128]{2,1,0:T(8,128)S(1)} all-gather(f32[1,12,128]{2,1,0:T(8,128)S(1)} %bitcast.246), channel_id=3, replica_groups=mesh['batch'=4,'seq'=8] {'seq'}, dimensions={0}, use_global_device_ids=true | all-gather | bytes 55296 | tf_op jit(solution)/shard_map/all_gather | solution.py:34
  92.5 30.5 %all-gather.2 = f32[8,12,128]{2,1,0:T(8,128)S(1)} all-gather(f32[1,12,128]{2,1,0:T(8,128)S(1)} %bitcast.243), channel_id=2, replica_groups=mesh['batch'=4,'seq'=8] {'seq'}, dimensions={0}, use_global_device_ids=true | all-gather | bytes 55296 | tf_op jit(solution)/shard_map/all_gather | solution.py:34
  174.3 35.2 %all-reduce.7.cloned.1.call-done = f32[128,12,64]{0,2,1:T(8,128)} async-done(((f32[128,12,64]{0,2,1:T(8,128)}), f32[128,12,64]{0,2,1:T(8,128)}) %all-reduce.7.cloned.1.call-update) | async-done | bytes 393232 | tf_op jit(solution)/shard_map/psum | solution.py:225
  234.1 15.2 %fusion.148 = (f32[4,12,256]{2,1,0:T(8,128)}, f32[4,12,256,512]{3,2,1,0:T(8,128)}) fusion(bf16[4,512,12,64]{1,3,2,0:T(8,128)(2,1)S(1)} %bitcast.194, bf16[4,256,12,64]{1,0,3,2:T(4,128)(2,1)} %reshape_reshape.3, pred[4,256,512]{2,1,0:T(8,128)(4,1)} %compare_and_fusion), kind=kOutput, calls=%fused_computation.278 | convolution fusion | flops 824168448 | bytes 30457856 | tf_op jit(solution)/shard_map/nqhe,nkhe->nhqk/dot_general | solution.py:181
  250.2 13.2 %exponential_reduce_fusion = f32[4,12,256]{2,1,0:T(8,128)S(1)} fusion(f32[4,12,256,128]{3,2,1,0:T(8,128)S(1)} %bitcast.193, f32[4,12,256,512]{3,2,1,0:T(8,128)} %get-tuple-element.352, f32[4,12,256]{2,1,0:T(8,128)S(1)} %is-finite_select_fusion), kind=kLoop, calls=%fused_computation.12 | loop fusion | flops 23580672 | bytes 31555584 | tf_op jit(solution)/shard_map/reduce_sum | solution.py:204
  278.9 11.4 fusion.43
  297.3 39.8 %multiply_convert_fusion.1 = (bf16[1152,3072]{1,0:T(8,128)(2,1)}, f32[1152,3072]{1,0:T(8,128)}, f32[1152,3072]{1,0:T(8,128)}) fusion(f32[3072]{0:T(1024)S(1)} %copy-done.107, bf16[1152,768]{0,1:T(8,128)(2,1)S(1)} %add_convert_fusion.1, bf16[768,3072]{1,0:T(8,128)(2,1)S(1)} %bitcast.248), kind=kOutput, calls=%fused_computation.19 | convolution fusion | flops 5669388288 | bytes 41889792 | tf_op jit(solution)/shard_map/dot_general | solution.py:71
  337.1 20.6 %add_convert_fusion = bf16[1152,3072]{1,0:T(8,128)(2,1)} fusion(f32[1152,3072]{1,0:T(8,128)} %get-tuple-element.322, bf16[3072,768]{1,0:T(8,128)(2,1)} %param.33, f32[1152,3072]{1,0:T(8,128)} %get-tuple-element.357, bf16[128,768]{0,1:T(8,128)(2,1)} %bitcast.231, bf16[1024,768]{0,1:T(8,128)(2,1)} %bitcast.202), kind=kOutput, calls=%fused_computation.18 | convolution fusion | flops 5488902144 | bytes 41877504 | tf_op jit(solution)/shard_map/dot_general | solution.py:75
  357.8 10.3 multiply_reduce_fusion.5
  379.3 9.7 fusion.14
  397.5 19.7 %psum.78 = f32[12,128]{1,0:T(8,128)S(1)} all-reduce(f32[12,128]{1,0:T(8,128)S(1)} %get-tuple-element.360), channel_id=1, replica_groups=mesh['batch'=4,'seq'=8] {'seq'}, use_global_device_ids=true, to_apply=%region_19.20 | all-reduce | flops 1536 | bytes 12288 | tf_op jit(solution)/shard_map/psum | solution.py:329
  430.9 10.1 fusion.85
  440.9 81.0 %multiply_convert_fusion = bf16[4,12,256,640]{3,2,1,0:T(8,128)(2,1)} fusion(f32[4,12,256,128]{3,2,1,0:T(8,128)} %convolution_bitcast_fusion, f32[4,12,256,512]{3,2,1,0:T(8,128)} %fusion.85, f32[4,12,256]{2,1,0:T(8,128)S(1)} %copy-done.72, f32[4,12,256,128]{3,2,1,0:T(8,128)} %get-tuple-element.354, f32[4,12,256,512]{3,2,1,0:T(8,128)} %get-tuple-element.352), kind=kOutput, calls=%fused_computation.8 | output fusion | flops 78656128 | bytes 78692352 | tf_op jit(solution)/shard_map/sub | solution.py:267
  547.7 10.5 fusion.42
  558.6 12.4 pad_maximum_fusion.3
  570.9 12.2 reduce_sum.409
  583.1 9.7 copy.179
  645.8 42.4 %all-reduce.9.cloned.1.call-done = (f32[128,1536]{1,0:T(8,128)}, f32[128,768]{1,0:T(8,128)}) async-done(((f32[128,1536]{1,0:T(8,128)}, f32[128,768]{1,0:T(8,128)}), (f32[128,1536]{1,0:T(8,128)}, f32[128,768]{1,0:T(8,128)})) %all-reduce.9.cloned.1.call-update) | async-done | bytes 1179664 | tf_op jit(solution)/shard_map/psum | solution.py:350
  691.7 9.6 fusion.30
  735.9 10.3 fusion.39
  794.8 122.9 %reduce-scatter.5.cloned.1.call-done = f32[24,2304]{1,0:T(8,128)} async-done(((f32[768,2304]{1,0:T(8,128)}), f32[24,2304]{1,0:T(8,128)}) %reduce-scatter.5.cloned.1.call-update) | async-done | bytes 221200 | tf_op jit(solution)/shard_map/reduce_scatter | solution.py:377
  920.0 138.8 %reduce-scatter.11.cloned.1.call-done = f32[96,768]{1,0:T(8,128)} async-done(((f32[3072,768]{1,0:T(8,128)}), f32[96,768]{1,0:T(8,128)}) %reduce-scatter.11.cloned.1.call-update) | async-done | bytes 294928 | tf_op jit(solution)/shard_map/reduce_scatter | solution.py:380
  1061.2 139.5 %reduce-scatter.9.cloned.1.call-done = f32[24,3072]{1,0:T(8,128)} async-done(((f32[768,3072]{1,0:T(8,128)}), f32[24,3072]{1,0:T(8,128)}) %reduce-scatter.9.cloned.1.call-update) | async-done | bytes 294928 | tf_op jit(solution)/shard_map/reduce_scatter | solution.py:379
  1205.8 41.4 %all-reduce.2 = (f32[2304]{0:T(1024)S(1)}, f32[4]{0:T(128)S(1)}, f32[768]{0:T(1024)S(1)}, f32[3072]{0:T(1024)S(1)}, f32[768]{0:T(1024)S(1)}, /*index=5*/f32[5,768]{1,0:T(8,128)S(1)}, f32[3072]{0:T(1024)S(1)}) all-reduce(f32[2304]{0:T(1024)S(1)} %get-tuple-element.273, ...), channel_id=1, replica_groups=mesh['batch'=4,'seq'=8] {'batch','seq'}, use_global_device_ids=true, to_apply=%region_28.29 | all-reduce | flops 13828 | bytes 110624 | tf_op jit(solution)/shard_map/psum | solution.py:394
  (458 shorter events, 378.7 us)
Async XLA Ops:
  7.2 202.2 %all-reduce.7.cloned.1.call-start = ((), (), s32[]{:S(2)}) async-start(), calls=%async_computation.4 | async-start | bytes 786432 | tf_op jit(solution)/shard_map/psum | solution.py:225
  10.0 283.5 %copy-start.24 = (f32[128,768]{0,1:T(8,128)}, f32[128,768]{0,1:T(8,128)S(1)}, u32[]{:S(2)}) copy-start(f32[128,768]{0,1:T(8,128)S(1)} %bitcast_convert_fusion.1) | copy-start | bytes 1179652
  15.2 278.3 %copy-start.2 = (f32[1024,768]{0,1:T(8,128)}, f32[1024,768]{0,1:T(8,128)S(1)}, u32[]{:S(2)}) copy-start(f32[1024,768]{0,1:T(8,128)S(1)} %bitcast_convert_fusion) | copy-start | bytes 9437188
  27.7 184.0 %collective-permute-start = (bf16[256,1536]{1,0:T(8,128)(2,1)}, bf16[256,1536]{1,0:T(8,128)(2,1)}, u32[]{:S(2)}, u32[]{:S(2)}) collective-permute-start(bf16[256,1536]{1,0:T(8,128)(2,1)} %get-tuple-element.328), channel_id=1, source_target_pairs={{0,1},{1,2},{2,3},{3,4},{4,5},{5,6},{6,7},{8,9},{9,10},{10,11},{11... | collective-permute-start | bytes 2359304 | tf_op jit(solution)/shard_map/ppermute | solution.py:27
  33.4 178.2 %collective-permute-start.1 = (bf16[256,1536]{1,0:T(8,128)(2,1)}, bf16[256,1536]{1,0:T(8,128)(2,1)}, u32[]{:S(2)}, u32[]{:S(2)}) collective-permute-start(bf16[256,1536]{1,0:T(8,128)(2,1)} %get-tuple-element.329), channel_id=1, source_target_pairs={{1,0},{2,1},{3,2},{4,3},{5,4},{6,5},{7,6},{9,8},{10,9},{11,10},{12... | collective-permute-start | bytes 2359304 | tf_op jit(solution)/shard_map/ppermute | solution.py:28
  131.5 77.9 %copy-start.68 = (f32[12,128]{1,0:T(8,128)}, f32[12,128]{1,0:T(8,128)S(1)}, u32[]{:S(2)}) copy-start(f32[12,128]{1,0:T(8,128)S(1)} %log_add_fusion.1) | copy-start | bytes 18436
  137.0 551.2 %all-reduce.9.cloned.1.call-start = ((), (), s32[]{:S(2)}) async-start(), calls=%async_computation.9 | async-start | bytes 2359296 | tf_op jit(solution)/shard_map/psum | solution.py:350
  296.0 41.1 %copy-start.85 = (f32[1152]{0:T(1024)}, f32[1152]{0:T(1024)S(1)}, u32[]{:S(2)}) copy-start(f32[1152]{0:T(1024)S(1)} %fusion.115) | copy-start | bytes 13828
  297.3 39.8 %copy-start.32 = (bf16[1152,768]{0,1:T(8,128)(2,1)}, bf16[1152,768]{0,1:T(8,128)(2,1)S(1)}, u32[]{:S(2)}) copy-start(bf16[1152,768]{0,1:T(8,128)(2,1)S(1)} %add_convert_fusion.1) | copy-start | bytes 5308420
  440.9 81.0 %copy-start.16 = (bf16[4,256,12,64]{1,0,3,2:T(4,128)(2,1)S(1)}, bf16[4,256,12,64]{1,0,3,2:T(4,128)(2,1)}, u32[]{:S(2)}) copy-start(bf16[4,256,12,64]{1,0,3,2:T(4,128)(2,1)} %reshape_reshape.3) | copy-start | bytes 4718596
  598.4 32.1 %collective-permute-start.2 = (bf16[256,1536]{1,0:T(8,128)(2,1)}, bf16[256,1536]{1,0:T(8,128)(2,1)}, u32[]{:S(2)}, u32[]{:S(2)}) collective-permute-start(bf16[256,1536]{1,0:T(8,128)(2,1)} %get-tuple-element.334), channel_id=1, source_target_pairs={{0,1},{1,2},{2,3},{3,4},{4,5},{5,6},{6,7},{8,9},{9,10},{10,11},{11... | collective-permute-start | bytes 2359304 | tf_op jit(solution)/shard_map/ppermute | solution.py:47
  601.9 190.6 %reduce-scatter.7.cloned.1.call-start = ((), (), s32[]{:S(2)}) async-start(), calls=%async_computation.6 | async-start | bytes 2433024 | tf_op jit(solution)/shard_map/reduce_scatter | solution.py:378
  619.7 17.8 %collective-permute-start.3 = (bf16[256,1536]{1,0:T(8,128)(2,1)}, bf16[256,1536]{1,0:T(8,128)(2,1)}, u32[]{:S(2)}, u32[]{:S(2)}) collective-permute-start(bf16[256,1536]{1,0:T(8,128)(2,1)} %get-tuple-element.333), channel_id=1, source_target_pairs={{1,0},{2,1},{3,2},{4,3},{5,4},{6,5},{7,6},{9,8},{10,9},{11,10},{12... | collective-permute-start | bytes 2359304 | tf_op jit(solution)/shard_map/ppermute | solution.py:47
  630.5 287.2 %reduce-scatter.5.cloned.1.call-start = ((), (), s32[]{:S(2)}) async-start(), calls=%async_computation.5 | async-start | bytes 7299072 | tf_op jit(solution)/shard_map/reduce_scatter | solution.py:377
  640.6 47.7 %copy-start.55 = (f32[128,768]{1,0:T(8,128)S(1)}, f32[128,768]{1,0:T(8,128)}, u32[]{:S(2)}) copy-start(f32[128,768]{1,0:T(8,128)} %copy.185) | copy-start | bytes 1179652
  645.8 45.8 %slice-start.6 = ((bf16[1152,768]{0,1:T(8,128)(2,1)}), bf16[1024,768]{0,1:T(8,128)(2,1)S(1)}, s32[]{:S(2)}) async-start(bf16[1152,768]{0,1:T(8,128)(2,1)} %copy-done.34), calls=%async_computation.16 | async-start | bytes 3145728 | tf_op jit(solution)/shard_map/slice | solution.py:145
  645.8 45.8 %copy-start.51 = (bf16[1024,768]{1,0:T(8,128)(2,1)S(1)}, bf16[1024,768]{1,0:T(8,128)(2,1)}, u32[]{:S(2)}) copy-start(bf16[1024,768]{1,0:T(8,128)(2,1)} %copy.182) | copy-start | bytes 4718596
  701.3 357.5 %reduce-scatter.11.cloned.1.call-start = ((), (), s32[]{:S(2)}) async-start(), calls=%async_computation.8 | async-start | bytes 9732096 | tf_op jit(solution)/shard_map/reduce_scatter | solution.py:380
  715.8 484.9 %reduce-scatter.9.cloned.1.call-start = ((), (), s32[]{:S(2)}) async-start(), calls=%async_computation.7 | async-start | bytes 9732096 | tf_op jit(solution)/shard_map/reduce_scatter | solution.py:379
  782.5 423.3 %copy-start.97 = (f32[3072]{0:T(1024)S(1)}, f32[3072]{0:T(1024)}, u32[]{:S(2)}) copy-start(f32[3072]{0:T(1024)} %convert_reduce_fusion) | copy-start | bytes 36868
  794.8 468.4 %copy-start.111 = (f32[24]{0:T(128)}, f32[24]{0:T(128)S(1)}, u32[]{:S(2)}) copy-start(f32[24]{0:T(128)S(1)} %get-tuple-element.314) | copy-start | bytes 292
  920.0 343.1 %copy-start.112 = (f32[24]{0:T(128)}, f32[24]{0:T(128)S(1)}, u32[]{:S(2)}) copy-start(f32[24]{0:T(128)S(1)} %get-tuple-element.312) | copy-start | bytes 292
  1061.2 201.9 %copy-start.113 = (f32[96]{0:T(128)}, f32[96]{0:T(128)S(1)}, u32[]{:S(2)}) copy-start(f32[96]{0:T(128)S(1)} %get-tuple-element.318) | copy-start | bytes 1156
  1203.1 60.0 %copy-start.114 = (f32[24]{0:T(128)}, f32[24]{0:T(128)S(1)}, u32[]{:S(2)}) copy-start(f32[24]{0:T(128)S(1)} %get-tuple-element.316) | copy-start | bytes 292
  (112 other events, 662.4 us)
Sparse Core Ops, SparseCore 0:
  137.1 72.2 all-reduce.6
  602.0 86.1 all-reduce.8
  694.1 98.3 reduce-scatter.6
  799.5 118.0 reduce-scatter.4
  924.0 134.8 reduce-scatter.10
  1066.1 134.5 reduce-scatter.8
where the time goes:
time: 1280 us; the launch traced here: 1270 us
  waiting for transfers between devices  486 us (38%)
  matrix products  249 us (19%)
  other arithmetic  223 us (17%)
  local copies, waits for them, and re-layouts  159 us (12%)
  blocking collectives  124 us (10%)
  between operations  18.7 us (1%)
    reduce_scatter x1, waiting for transfers between devices, body(): lax.psum_scatter(grad_up, ('batch', 'seq'), scatter_dimension=0, tiled=True)  140 us
    reduce_scatter x1, waiting for transfers between devices, body(): lax.psum_scatter(grad_down, ('batch', 'seq'), scatter_dimension=0, tiled=...  139 us
    reduce_scatter x1, waiting for transfers between devices, body(): lax.psum_scatter(grad_qkv, ('batch', 'seq'), scatter_dimension=0, tiled=T...  123 us
    sub x1, other arithmetic, body(): score_grad_low = (weights_again * (weight_grad - row_inner)).astype(bf16)  81 us
    all_gather x2, blocking collectives, joined(): gathered = jax.tree.map(lambda a: lax.all_gather(a, axis), part)  62.5 us
    dot_general x4, matrix products, dense(): return jnp.dot(left_rows, right_rows, preferred_element_type=jnp.float32)  57.1 us
    psum x1, waiting for transfers between devices, body(): lax.psum((glob_query_part.reshape(glob_count, model_width), glob_pair_par...  42.4 us
    psum x1, blocking collectives, body(): lax.psum((col_parts[0], col_parts[1], col_parts[2], col_parts[3], row_tot...  41.4 us
  transfers between devices with their start and end apart: 10, of which 7 were waited for; matrix products, arithmetic and copies ran while one was open for 17% of the time, Pallas kernels for 0%

commit v1 on v0

--- a/solution.py
+++ b/solution.py
@@ -30,15 +30,56 @@
     return x
 
 
-def joined(part, axis, combine):
-    gathered = jax.tree.map(lambda a: lax.all_gather(a, axis), part)
-
-    def take(source):
-        return jax.tree.map(lambda a: lax.dynamic_index_in_dim(a, source, 0, False), gathered)
-
-    return lax.fori_loop(
-        1, lax.axis_size(axis), lambda source, state: combine(state, take(source)), take(0)
-    )
+def bits_of(axis):
+    size = lax.axis_size(axis)
+    assert size & (size - 1) == 0
+    return [(axis, 1 << k) for k in range(size.bit_length() - 1)]
+
+
+def side_of(axis, bit):
+    return (lax.axis_index(axis) // bit) % 2
+
+
+def swapped(values, axis, bit):
+    return lax.ppermute(values, axis, [(i, i ^ bit) for i in range(lax.axis_size(axis))])
+
+
+def summed(parts, bits):
+    leaves, tree = jax.tree.flatten(parts)
+    flat = jnp.concatenate([leaf.reshape(-1) for leaf in leaves])
+    count = flat.shape[0]
+    flat = jnp.pad(flat, (0, -count % 1024)).reshape(-1, 128)
+    for axis, bit in bits:
+        flat = flat + swapped(flat, axis, bit)
+    flat = flat.reshape(-1)
+    out, place = [], 0
+    for leaf in leaves:
+        out.append(flat[place : place + leaf.size].reshape(leaf.shape))
+        place += leaf.size
+    return jax.tree.unflatten(tree, out)
+
+
+def scattered(grad, order):
+    labels = bits_of("batch")[::-1] + bits_of("seq")[::-1]
+    held = grad.reshape((2,) * len(labels) + (-1, grad.shape[-1]))
+    for axis, bit in order:
+        dim = labels.index((axis, bit))
+        labels.pop(dim)
+        mine = side_of(axis, bit)
+        sent = lax.dynamic_index_in_dim(held, 1 - mine, dim, False).astype(jnp.bfloat16)
+        kept = lax.dynamic_index_in_dim(held, mine, dim, False).astype(jnp.float32)
+        held = kept + swapped(sent, axis, bit).astype(jnp.float32)
+    return held
+
+
+def joined(state, axis, combine):
+    for _, bit in bits_of(axis):
+        other = jax.tree.map(lambda a: swapped(a, axis, bit), state)
+        upper = side_of(axis, bit) == 1
+        first = jax.tree.map(lambda a, b: jnp.where(upper, b, a), state, other)
+        second = jax.tree.map(lambda a, b: jnp.where(upper, a, b), state, other)
+        state = combine(first, second)
+    return state
 
 
 def from_behind(block, axis, distance):
@@ -222,7 +263,7 @@
     token_weights_low = jnp.exp(to_tokens - glob_total).astype(bf16)
     self_weights_low = jnp.exp(to_globs - glob_total).astype(bf16)
     glob_part = jnp.einsum("hgk,khe->ghe", token_weights_low, value_own, preferred_element_type=f32)
-    glob_att = lax.psum(glob_part, "seq")
+    glob_att = summed(glob_part, bits_of("seq"))
     glob_att = glob_att + jnp.einsum(
         "hgj,jhe->ghe", self_weights_low, glob_value, preferred_element_type=f32
     )
@@ -326,7 +367,7 @@
         "ghe,jhe->hgj", glob_heads_grad, glob_value, preferred_element_type=f32
     )
     part_inner = jnp.sum(token_weights * token_weight_grad, axis=-1)
-    glob_inner = lax.psum(part_inner, "seq") + jnp.sum(self_weights * self_weight_grad, axis=-1)
+    glob_inner = summed(part_inner, bits_of("seq")) + jnp.sum(self_weights * self_weight_grad, axis=-1)
     token_score_low = (token_weights * (token_weight_grad - glob_inner[..., None])).astype(bf16)
     self_score_low = (self_weights * (self_weight_grad - glob_inner[..., None])).astype(bf16)
     glob_query_part = (
@@ -347,8 +388,8 @@
         ],
         axis=-1,
     )
-    query_sum, pair_sum = lax.psum(
-        (glob_query_part.reshape(glob_count, model_width), glob_pair_part), "seq"
+    query_sum, pair_sum = summed(
+        (glob_query_part.reshape(glob_count, model_width), glob_pair_part), bits_of("seq")
     )
     glob_query_grad = query_sum + (
         jnp.einsum("hgj,jhe->ghe", self_score_low, glob_key, preferred_element_type=f32)
@@ -373,11 +414,14 @@
     row_grad = mixed_grad + norm_backward(rows_all, vec_params[0], vec_params[1], d_normed)
     gain_one, shift_one = norm_terms(counted(rows_all), counted(d_normed))
     vec_grad_part = jnp.stack([gain_one, shift_one, gain_two, shift_two, bias_two_grad])
+    batch_bits, seq_bits = bits_of("batch"), bits_of("seq")
+    order_one = batch_bits + seq_bits
+    order_two = batch_bits[:1] + seq_bits[:1] + batch_bits[1:] + seq_bits[1:]
     shards = (
-        lax.psum_scatter(grad_qkv, ("batch", "seq"), scatter_dimension=0, tiled=True),
-        lax.psum_scatter(grad_out, ("batch", "seq"), scatter_dimension=0, tiled=True),
-        lax.psum_scatter(grad_up, ("batch", "seq"), scatter_dimension=0, tiled=True),
-        lax.psum_scatter(grad_down, ("batch", "seq"), scatter_dimension=0, tiled=True),
+        scattered(grad_qkv, order_two),
+        scattered(grad_out, order_two),
+        scattered(grad_up, order_two),
+        scattered(grad_down, order_one),
     )
     decay_rate = 1.0 - STEP ** (-0.8)
     owner_index = lax.axis_index(("batch", "seq"))
@@ -391,7 +435,7 @@
     ]
     col_parts = [jnp.sum(square, axis=0) for square in squares]
     row_totals = jnp.stack([jnp.sum(row_new) for row_new in row_news])
-    stats = lax.psum(
+    stats = summed(
         (
             col_parts[0],
             col_parts[1],
@@ -401,7 +445,7 @@
             vec_grad_part,
             bias_grad_part,
         ),
-        ("batch", "seq"),
+        batch_bits + seq_bits,
     )
     updates = []
     for matrix_index in range(4):

time: 1280 us -> 869 us (0.68)
  waiting for transfers between devices: 486 us -> 126 us
  blocking collectives: 124 us -> 0 us
  starting transfers between devices: 11.2 us -> 58.4 us
  local copies, waits for them, and re-layouts: 159 us -> 184 us
  other arithmetic: 223 us -> 241 us
  between operations: 18.7 us -> 5.42 us
    reduce_scatter x4 -> x0, waiting for transfers between devices: 404 us -> none  [the longest x1 140 us: body(): lax.psum_scatter(grad_up, ('batch', 'seq'), scatter_dimension=0, tiled=True)]
    ppermute x0 -> x40, waiting for transfers between devices: none -> 126 us  [swapped(): lax.ppermute(values, axis, [(i, i ^ bit) for i in range(lax.axis_size(axi...]
    psum x2 -> x0, waiting for transfers between devices: 77.5 us -> none  [the longest x1 42.4 us: body(): lax.psum((glob_query_part.reshape(glob_count, model_width), glob_pair_par...]
    all_gather x2 -> x0, blocking collectives: 62.5 us -> none  [joined(): gathered = jax.tree.map(lambda a: lax.all_gather(a, axis), part)]
    psum x2 -> x0, blocking collectives: 61.1 us -> none  [the longest x1 41.4 us: body(): lax.psum((col_parts[0], col_parts[1], col_parts[2], col_parts[3], row_tot...]
    ppermute x0 -> x40, starting transfers between devices: none -> 44.2 us  [swapped(): lax.ppermute(values, axis, [(i, i ^ bit) for i in range(lax.axis_size(axi...]
    add x1 -> x30, other arithmetic: 0.01 us -> 25.7 us  [the longest x16 15.2 us: scattered(): held = kept + swapped(sent, axis, bit).astype(jnp.float32)]
    unnamed x256 -> x314, local copies, waits for them, and re-layouts: 40.7 us -> 41 us
  transfers between devices with their start and end apart: 10 -> 44, of which waited for: 7 -> 19; matrix products, arithmetic and copies ran while one was open for 17% -> 42% of each run, Pallas kernels for 0% -> 0%
where the time goes in v1:
time: 869 us; the launch traced here: 861 us
  matrix products  246 us (28%)
  other arithmetic  241 us (28%)
  local copies, waits for them, and re-layouts  184 us (21%)
  waiting for transfers between devices  126 us (14%)
  starting transfers between devices  58.4 us (7%)
    ppermute x40, waiting for transfers between devices, swapped(): lax.ppermute(values, axis, [(i, i ^ bit) for i in range(lax.axis_size(axi...  126 us
    sub x1, other arithmetic, body(): score_grad_low = (weights_again * (weight_grad - row_inner)).astype(bf16)  80.9 us
    dot_general x4, matrix products, dense(): return jnp.dot(left_rows, right_rows, preferred_element_type=jnp.float32)  56.3 us
    ppermute x40, starting transfers between devices, swapped(): lax.ppermute(values, axis, [(i, i ^ bit) for i in range(lax.axis_size(axi...  44.2 us
    dot_general x4, matrix products, dense_back(): lax.dot_general(grad_rows, matrix, (((1,), (1,)), ((), ())), preferred_el...  41.1 us
    unnamed x314, local copies, waits for them, and re-layouts  41 us
    dot_general x4, matrix products, outer_sum(): lax.dot_general(input_rows, grad_rows, (((0,), (0,)), ((), ())), preferre...  23.5 us
  transfers between devices with their start and end apart: 44, of which 19 were waited for; matrix products, arithmetic and copies ran while one was open for 42% of the time, Pallas kernels for 0%

profile of v1, /device:TPU:0, one launch (start us, length us, event | category | flops | bytes accessed | tf_op | source)
XLA Modules:
  0.0 861.5 jit_solution(14195038209491072292)
XLA Ops:
  131.4 7.0 broadcast_in_dim.58
  143.3 15.2 %fusion.184 = (f32[4,12,256]{2,1,0:T(8,128)}, f32[4,12,256,512]{3,2,1,0:T(8,128)}) fusion(bf16[4,512,12,64]{1,3,2,0:T(8,128)(2,1)S(1)} %bitcast.295, bf16[4,256,12,64]{1,0,3,2:T(4,128)(2,1)} %reshape_reshape.9, pred[4,256,512]{2,1,0:T(8,128)(4,1)} %compare_and_fusion), kind=kOutput, calls=%fused_computation.368 | convolution fusion | flops 824168448 | bytes 30457856 | tf_op jit(solution)/shard_map/nqhe,nkhe->nhqk/dot_general | solution.py:222
  159.4 13.2 %exponential_reduce_fusion = f32[4,12,256]{2,1,0:T(8,128)S(1)} fusion(f32[4,12,256,128]{3,2,1,0:T(8,128)S(1)} %bitcast.294, f32[4,12,256,512]{3,2,1,0:T(8,128)} %get-tuple-element.207, f32[4,12,256]{2,1,0:T(8,128)S(1)} %is-finite_select_fusion), kind=kLoop, calls=%fused_computation.7 | loop fusion | flops 23580672 | bytes 31555584 | tf_op jit(solution)/shard_map/reduce_sum | solution.py:245
  174.8 8.2 fusion.36
  190.7 11.4 %fusion.41 = bf16[4,256,12,64]{1,3,2,0:T(8,128)(2,1)} fusion(f32[12,64,4,256]{3,1,0,2:T(8,128)} %fusion.164, bf16[4,512,12,64]{1,3,2,0:T(8,128)(2,1)} %bitcast.297, bf16[4,12,256,640]{3,2,1,0:T(8,128)(2,1)} %fusion.36), kind=kOutput, calls=%fused_computation.103 | convolution fusion | flops 806879232 | bytes 20447232 | tf_op jit(solution)/shard_map/nhqk,nkhe->nqhe/dot_general | solution.py:247
  222.4 37.1 %multiply_convert_fusion.1 = (bf16[1152,3072]{1,0:T(8,128)(2,1)S(1)}, f32[1152,3072]{1,0:T(8,128)}, f32[1152,3072]{1,0:T(8,128)}) fusion(f32[3072]{0:T(1024)S(1)} %copy-done.123, bf16[1152,768]{0,1:T(8,128)(2,1)S(1)} %add_convert_fusion.1, bf16[768,3072]{1,0:T(8,128)(2,1)S(1)} %bitcast.364), kind=kOutput, calls=%fused_computation.14 | convolution fusion | flops 5669388288 | bytes 41889792 | tf_op jit(solution)/shard_map/dot_general | solution.py:112
  265.3 21.0 %add_convert_fusion = bf16[1152,3072]{1,0:T(8,128)(2,1)} fusion(f32[1152,3072]{1,0:T(8,128)} %get-tuple-element.171, bf16[3072,768]{1,0:T(8,128)(2,1)} %param.31, f32[1152,3072]{1,0:T(8,128)} %get-tuple-element.212, bf16[128,768]{0,1:T(8,128)(2,1)} %bitcast.342, bf16[1024,768]{0,1:T(8,128)(2,1)} %bitcast.305), kind=kOutput, calls=%fused_computation.13 | convolution fusion | flops 5488902144 | bytes 41877504 | tf_op jit(solution)/shard_map/dot_general | solution.py:116
  288.5 10.5 %multiply_reduce_fusion.5 = (f32[1152]{0:T(1024)S(1)}, f32[1152,768]{0,1:T(8,128)S(1)}) fusion(f32[1152,768]{0,1:T(8,128)S(1)} %copy-done.5, f32[768]{0:T(1024)S(1)} %copy-done.111, f32[1152]{0:T(1024)S(1)} %copy-done.90, bf16[1152,3072]{1,0:T(8,128)(2,1)} %add_convert_fusion, bf16[768,3072]{1,0:T(8,128)(2,1)} %param.30), kind=kOutput, calls=%fused_computation.89 | convolution fusion | flops 5439355904 | bytes 18886656 | tf_op jit(solution)/shard_map/dot_general | solution.py:116
  315.3 9.7 %fusion.12 = f32[4,12,64,512]{3,2,1,0:T(8,128)} fusion(bf16[4,12,256,640]{3,2,1,0:T(8,128)(2,1)} %fusion.36, bf16[4,256,12,64]{1,0,3,2:T(4,128)(2,1)S(1)} %reshape.461), kind=kOutput, calls=%fused_computation.34 | convolution fusion | flops 805306368 | bytes 20447232 | tf_op jit(solution)/shard_map/nhqk,nqhe->nkhe/dot_general | solution.py:324
  338.8 10.1 %fusion.86 = f32[4,12,256,512]{3,2,1,0:T(8,128)} fusion(bf16[4,512,12,64]{1,3,2,0:T(8,128)(2,1)S(1)} %bitcast.298, bf16[4,256,12,64]{1,0,3,2:T(4,128)(2,1)S(1)} %reshape.461), kind=kOutput, calls=%fused_computation.160 | convolution fusion | flops 805306368 | bytes 29884416 | tf_op jit(solution)/shard_map/nqhe,nkhe->nhqk/dot_general | solution.py:302
  349.0 80.9 %multiply_convert_fusion = bf16[4,12,256,640]{3,2,1,0:T(8,128)(2,1)} fusion(f32[4,12,256,128]{3,2,1,0:T(8,128)} %convolution_bitcast_fusion, f32[4,12,256,512]{3,2,1,0:T(8,128)} %fusion.86, f32[4,12,256]{2,1,0:T(8,128)S(1)} %copy-done.81, f32[4,12,256,128]{3,2,1,0:T(8,128)} %get-tuple-element.209, f32[4,12,256,512]{3,2,1,0:T(8,128)} %get-tuple-element.207), kind=kOutput, calls=%fused_computation.3 | output fusion | flops 78656128 | bytes 78692352 | tf_op jit(solution)/shard_map/sub | solution.py:308
  438.2 9.7 %broadcast_multiply_fusion = f32[4,12,64,512]{3,2,1,0:T(8,128)} fusion(bf16[4,12,256,640]{3,2,1,0:T(8,128)(2,1)} %multiply_convert_fusion, bf16[4,256,12,64]{1,0,3,2:T(4,128)(2,1)S(1)} %copy-done.16), kind=kOutput, calls=%fused_computation.108 | convolution fusion | flops 806879232 | bytes 20447232 | tf_op jit(solution)/shard_map/nhqk,nqhe->nkhe/dot_general | solution.py:319
  468.1 8.5 fusion.32
  485.6 11.4 %fusion.40 = bf16[4,256,12,64]{1,3,2,0:T(8,128)(2,1)} fusion(f32[12,64,4,256]{3,1,0,2:T(8,128)} %fusion.162, bf16[4,512,12,64]{1,3,2,0:T(8,128)(2,1)} %bitcast.296, bf16[4,12,256,640]{3,2,1,0:T(8,128)(2,1)} %multiply_convert_fusion), kind=kOutput, calls=%fused_computation.101 | convolution fusion | flops 807665664 | bytes 20447232 | tf_op jit(solution)/shard_map/nhqk,nkhe->nqhe/dot_general | solution.py:309
  497.4 12.4 %pad_maximum_fusion.3 = f32[6,512,1536]{1,2,0:T(8,128)} fusion(f32[1,512,1536]{1,2,0:T(8,128)S(1)} %broadcast_in_dim.118, f32[4,512,768]{1,2,0:T(8,128)} %bitcast.300, f32[4,512,768]{1,2,0:T(8,128)} %bitcast.301), kind=kLoop, calls=%fused_computation.10 | loop fusion | flops 14155776 | bytes 34603008 | tf_op jit(solution)/shard_map/concatenate | solution.py:134
  509.8 12.2 %reduce_sum.409 = f32[3,512,1536]{1,2,0:T(8,128)} reduce(f32[3,2,512,1536]{2,3,1,0:T(8,128)} %bitcast.292, f32[]{:T(128)} %constant.458.clone.1), dimensions={1}, to_apply=%region_14.15 | reduce | flops 2359296 | bytes 28311556 | tf_op jit(solution)/shard_map/reduce_sum | solution.py:136
  522.0 9.7 %copy.199 = f32[3,512,1536]{2,1,0:T(8,128)} copy(f32[3,512,1536]{1,2,0:T(8,128)} %reduce_sum.409) | data formatting | bytes 18874368 | tf_op jit(solution)/shard_map/reduce_sum | solution.py:136
  597.1 7.2 collective-permute-done.25
  624.8 7.0 collective-permute-done.16
  643.2 15.2 %collective-permute-done.17 = f32[2304,128]{1,0:T(8,128)S(1)} collective-permute-done((f32[2304,128]{1,0:T(8,128)S(1)}, f32[2304,128]{1,0:T(8,128)S(1)}, u32[]{:S(2)}, u32[]{:S(2)}) %collective-permute-start.17) | collective-permute-done | bytes 1179680 | tf_op jit(solution)/shard_map/ppermute | solution.py:44
  672.0 38.1 %collective-permute-done.18 = f32[2304,128]{1,0:T(8,128)S(1)} collective-permute-done((f32[2304,128]{1,0:T(8,128)S(1)}, f32[2304,128]{1,0:T(8,128)S(1)}, u32[]{:S(2)}, u32[]{:S(2)}) %collective-permute-start.18) | collective-permute-done | bytes 1179680 | tf_op jit(solution)/shard_map/ppermute | solution.py:44
  719.8 7.9 multiply_reduce_fusion.4
  768.0 15.1 %collective-permute-done.20 = bf16[2,2,2,24,2304]{4,3,1,2,0:T(8,128)(2,1)S(1)} collective-permute-done((bf16[2,2,2,24,2304]{4,3,1,2,0:T(8,128)(2,1)S(1)}, bf16[2,2,2,24,2304]{4,3,1,2,0:T(8,128)(2,1)S(1)}, u32[]{:S(2)}, u32[]{:S(2)}) %collective-permute-start.20) | collective-permute-done | bytes 884768 | tf_op jit(solution)/shard_map/ppermute | solution.py:44
  813.4 10.4 %fusion.37 = bf16[1152,768]{0,1:T(8,128)(2,1)S(1)} fusion(f32[1152,768]{0,1:T(8,128)S(1)} %copy-done.6, bf16[1152,3072]{1,0:T(8,128)(2,1)} %copy-done.34, bf16[3072,768]{1,0:T(8,128)(2,1)} %param.31, f32[768]{0:T(1024)} %get-tuple-element.142), kind=kOutput, calls=%fused_computation.95 | convolution fusion | flops 5438472192 | bytes 17107968 | tf_op jit(solution)/shard_map/dot_general | solution.py:112
  (633 shorter events, 467.0 us)
Async XLA Ops:
  18.9 101.6 %collective-permute-start = (bf16[256,1536]{1,0:T(8,128)(2,1)}, bf16[256,1536]{1,0:T(8,128)(2,1)}, u32[]{:S(2)}, u32[]{:S(2)}) collective-permute-start(bf16[256,1536]{1,0:T(8,128)(2,1)} %get-tuple-element.181), channel_id=1, source_target_pairs={{0,1},{1,2},{2,3},{3,4},{4,5},{5,6},{6,7},{8,9},{9,10},{10,11},{11... | collective-permute-start | bytes 2359304 | tf_op jit(solution)/shard_map/ppermute | solution.py:27
  24.7 95.9 %collective-permute-start.1 = (bf16[256,1536]{1,0:T(8,128)(2,1)}, bf16[256,1536]{1,0:T(8,128)(2,1)}, u32[]{:S(2)}, u32[]{:S(2)}) collective-permute-start(bf16[256,1536]{1,0:T(8,128)(2,1)} %get-tuple-element.182), channel_id=1, source_target_pairs={{1,0},{2,1},{3,2},{4,3},{5,4},{6,5},{7,6},{9,8},{10,9},{11,10},{12... | collective-permute-start | bytes 2359304 | tf_op jit(solution)/shard_map/ppermute | solution.py:28
  37.3 28.5 %collective-permute-start.2 = (f32[12,128]{1,0:T(8,128)S(1)}, f32[12,128]{1,0:T(8,128)}, u32[]{:S(2)}, u32[]{:S(2)}) collective-permute-start(f32[12,128]{1,0:T(8,128)S(1)} %get-tuple-element.204), channel_id=1, source_target_pairs={{0,1},{1,0},{2,3},{3,2},{4,5},{5,4},{6,7},{7,6},{8,9},{9,8},{10,11... | collective-permute-start | bytes 18440 | tf_op jit(solution)/shard_map/ppermute | solution.py:44
  42.2 23.6 %collective-permute-start.5 = (f32[12,128]{1,0:T(8,128)}, f32[12,128]{1,0:T(8,128)}, u32[]{:S(2)}, u32[]{:S(2)}) collective-permute-start(f32[12,128]{1,0:T(8,128)} %exponential_reduce_fusion.1), channel_id=1, source_target_pairs={{0,1},{1,0},{2,3},{3,2},{4,5},{5,4},{6,7},{7,6},{8,9},{9,8},{10,11... | collective-permute-start | bytes 18440 | tf_op jit(solution)/shard_map/ppermute | solution.py:44
  76.6 17.3 %collective-permute-start.4 = (f32[12,128]{1,0:T(8,128)S(1)}, f32[12,128]{1,0:T(8,128)}, u32[]{:S(2)}, u32[]{:S(2)}) collective-permute-start(f32[12,128]{1,0:T(8,128)S(1)} %get-tuple-element.173), channel_id=1, source_target_pairs={{0,4},{1,5},{2,6},{3,7},{4,0},{5,1},{6,2},{7,3},{8,12},{9,13},{10,... | collective-permute-start | bytes 18440 | tf_op jit(solution)/shard_map/ppermute | solution.py:44
  118.9 68.9 %collective-permute-start.9 = (f32[768,128]{1,0:T(8,128)}, f32[768,128]{1,0:T(8,128)}, u32[]{:S(2)}, u32[]{:S(2)}) collective-permute-start(f32[768,128]{1,0:T(8,128)} %add.486), channel_id=1, source_target_pairs={{0,2},{1,3},{2,0},{3,1},{4,6},{5,7},{6,4},{7,5},{8,10},{9,11},{10,... | collective-permute-start | bytes 1179656 | tf_op jit(solution)/shard_map/ppermute | solution.py:44
  461.4 170.8 %collective-permute-start.34 = (bf16[2,2,2,2,96,768]{5,4,1,2,3,0:T(8,128)(2,1)}, bf16[2,2,2,2,96,768]{5,4,1,2,3,0:T(8,128)(2,1)}, u32[]{:S(2)}, u32[]{:S(2)}) collective-permute-start(bf16[2,2,2,2,96,768]{5,4,1,2,3,0:T(8,128)(2,1)} %fusion.47), channel_id=1, source_target_pairs={{0,8},{8,0},{16,24},{24,16},{1,9},{9,1},{17,25},{25,17},{2,10},{10... | collective-permute-start | bytes 7077896 | tf_op jit(solution)/shard_map/ppermute | solution.py:44
  482.0 155.5 %collective-permute-start.29 = (bf16[2,2,2,2,24,3072]{5,4,1,2,0,3:T(8,128)(2,1)}, bf16[2,2,2,2,24,3072]{5,4,1,2,0,3:T(8,128)(2,1)}, u32[]{:S(2)}, u32[]{:S(2)}) collective-permute-start(bf16[2,2,2,2,24,3072]{5,4,1,2,0,3:T(8,128)(2,1)} %fusion.46), channel_id=1, source_target_pairs={{0,8},{8,0},{16,24},{24,16},{1,9},{9,1},{17,25},{25,17},{2,10},{10... | collective-permute-start | bytes 7077896 | tf_op jit(solution)/shard_map/ppermute | solution.py:44
  483.1 57.8 %collective-permute-start.13 = (f32[16,128]{1,0:T(8,128)}, f32[16,128]{1,0:T(8,128)}, u32[]{:S(2)}, u32[]{:S(2)}) collective-permute-start(f32[16,128]{1,0:T(8,128)} %pad_bitcast_fusion.1), channel_id=1, source_target_pairs={{0,1},{1,0},{2,3},{3,2},{4,5},{5,4},{6,7},{7,6},{8,9},{9,8},{10,11... | collective-permute-start | bytes 24584 | tf_op jit(solution)/shard_map/ppermute | solution.py:44
  546.1 19.9 %collective-permute-start.15 = (f32[16,128]{1,0:T(8,128)S(1)}, f32[16,128]{1,0:T(8,128)S(1)}, u32[]{:S(2)}, u32[]{:S(2)}) collective-permute-start(f32[16,128]{1,0:T(8,128)S(1)} %fusion.230), channel_id=1, source_target_pairs={{0,4},{1,5},{2,6},{3,7},{4,0},{5,1},{6,2},{7,3},{8,12},{9,13},{10,... | collective-permute-start | bytes 24584 | tf_op jit(solution)/shard_map/ppermute | solution.py:44
  550.9 42.9 %collective-permute-start.24 = (bf16[2,2,2,2,24,768]{5,4,1,2,0,3:T(8,128)(2,1)}, bf16[2,2,2,2,24,768]{5,4,1,2,0,3:T(8,128)(2,1)}, u32[]{:S(2)}, u32[]{:S(2)}) collective-permute-start(bf16[2,2,2,2,24,768]{5,4,1,2,0,3:T(8,128)(2,1)} %fusion.102), channel_id=1, source_target_pairs={{0,8},{8,0},{16,24},{24,16},{1,9},{9,1},{17,25},{25,17},{2,10},{10... | collective-permute-start | bytes 1769480 | tf_op jit(solution)/shard_map/ppermute | solution.py:44
  558.6 53.4 %collective-permute-start.12 = (bf16[256,1536]{1,0:T(8,128)(2,1)}, bf16[256,1536]{1,0:T(8,128)(2,1)}, u32[]{:S(2)}, u32[]{:S(2)}) collective-permute-start(bf16[256,1536]{1,0:T(8,128)(2,1)} %get-tuple-element.186), channel_id=1, source_target_pairs={{1,0},{2,1},{3,2},{4,3},{5,4},{6,5},{7,6},{9,8},{10,9},{11,10},{12... | collective-permute-start | bytes 2359304 | tf_op jit(solution)/shard_map/ppermute | solution.py:88
  566.0 40.4 %collective-permute-start.11 = (bf16[256,1536]{1,0:T(8,128)(2,1)}, bf16[256,1536]{1,0:T(8,128)(2,1)}, u32[]{:S(2)}, u32[]{:S(2)}) collective-permute-start(bf16[256,1536]{1,0:T(8,128)(2,1)} %get-tuple-element.187), channel_id=1, source_target_pairs={{0,1},{1,2},{2,3},{3,4},{4,5},{5,6},{6,7},{8,9},{9,10},{10,11},{11... | collective-permute-start | bytes 2359304 | tf_op jit(solution)/shard_map/ppermute | solution.py:88
  604.4 27.4 %collective-permute-start.16 = (f32[2304,128]{1,0:T(8,128)S(1)}, f32[2304,128]{1,0:T(8,128)S(1)}, u32[]{:S(2)}, u32[]{:S(2)}) collective-permute-start(f32[2304,128]{1,0:T(8,128)S(1)} %maximum_bitcast_fusion), channel_id=1, source_target_pairs={{0,1},{1,0},{2,3},{3,2},{4,5},{5,4},{6,7},{7,6},{8,9},{9,8},{10,11... | collective-permute-start | bytes 3538952 | tf_op jit(solution)/shard_map/ppermute | solution.py:44
  631.9 26.5 %collective-permute-start.17 = (f32[2304,128]{1,0:T(8,128)S(1)}, f32[2304,128]{1,0:T(8,128)S(1)}, u32[]{:S(2)}, u32[]{:S(2)}) collective-permute-start(f32[2304,128]{1,0:T(8,128)S(1)} %fusion.161), channel_id=1, source_target_pairs={{0,2},{1,3},{2,0},{3,1},{4,6},{5,7},{6,4},{7,5},{8,10},{9,11},{10,... | collective-permute-start | bytes 3538952 | tf_op jit(solution)/shard_map/ppermute | solution.py:44
  636.0 26.2 %collective-permute-start.35 = (bf16[2,2,2,96,768]{4,3,0,1,2:T(8,128)(2,1)S(1)}, bf16[2,2,2,96,768]{4,3,0,1,2:T(8,128)(2,1)S(1)}, u32[]{:S(2)}, u32[]{:S(2)}) collective-permute-start(bf16[2,2,2,96,768]{4,3,0,1,2:T(8,128)(2,1)S(1)} %fusion.97), channel_id=1, source_target_pairs={{0,16},{8,24},{16,0},{24,8},{1,17},{9,25},{17,1},{25,9},{2,18},{10... | collective-permute-start | bytes 3538952 | tf_op jit(solution)/shard_map/ppermute | solution.py:44
  641.4 29.0 %collective-permute-start.30 = (bf16[2,2,2,24,3072]{4,3,1,2,0:T(8,128)(2,1)S(1)}, bf16[2,2,2,24,3072]{4,3,1,2,0:T(8,128)(2,1)S(1)}, u32[]{:S(2)}, u32[]{:S(2)}) collective-permute-start(bf16[2,2,2,24,3072]{4,3,1,2,0:T(8,128)(2,1)S(1)} %fusion.96), channel_id=1, source_target_pairs={{0,1},{1,0},{2,3},{3,2},{4,5},{5,4},{6,7},{7,6},{8,9},{9,8},{10,11... | collective-permute-start | bytes 3538952 | tf_op jit(solution)/shard_map/ppermute | solution.py:44
  658.6 51.5 %collective-permute-start.18 = (f32[2304,128]{1,0:T(8,128)S(1)}, f32[2304,128]{1,0:T(8,128)S(1)}, u32[]{:S(2)}, u32[]{:S(2)}) collective-permute-start(f32[2304,128]{1,0:T(8,128)S(1)} %fusion.229), channel_id=1, source_target_pairs={{0,4},{1,5},{2,6},{3,7},{4,0},{5,1},{6,2},{7,3},{8,12},{9,13},{10,... | collective-permute-start | bytes 3538952 | tf_op jit(solution)/shard_map/ppermute | solution.py:44
  663.5 84.5 %collective-permute-start.36 = (bf16[2,2,96,768]{3,2,0,1:T(8,128)(2,1)}, bf16[2,2,96,768]{3,2,0,1:T(8,128)(2,1)}, u32[]{:S(2)}, u32[]{:S(2)}) collective-permute-start(bf16[2,2,96,768]{3,2,0,1:T(8,128)(2,1)} %fusion.101), channel_id=1, source_target_pairs={{0,1},{1,0},{2,3},{3,2},{4,5},{5,4},{6,7},{7,6},{8,9},{9,8},{10,11... | collective-permute-start | bytes 1769480 | tf_op jit(solution)/shard_map/ppermute | solution.py:44
  671.8 78.4 %collective-permute-start.31 = (bf16[2,2,24,3072]{3,2,0,1:T(8,128)(2,1)}, bf16[2,2,24,3072]{3,2,0,1:T(8,128)(2,1)}, u32[]{:S(2)}, u32[]{:S(2)}) collective-permute-start(bf16[2,2,24,3072]{3,2,0,1:T(8,128)(2,1)} %fusion.100), channel_id=1, source_target_pairs={{0,16},{8,24},{16,0},{24,8},{1,17},{9,25},{17,1},{25,9},{2,18},{10... | collective-permute-start | bytes 1769480 | tf_op jit(solution)/shard_map/ppermute | solution.py:44
  739.3 21.1 %collective-permute-start.19 = (bf16[2,2,2,2,24,2304]{5,4,1,2,0,3:T(8,128)(2,1)}, bf16[2,2,2,2,24,2304]{5,4,1,2,0,3:T(8,128)(2,1)}, u32[]{:S(2)}, u32[]{:S(2)}) collective-permute-start(bf16[2,2,2,2,24,2304]{5,4,1,2,0,3:T(8,128)(2,1)} %fusion.57), channel_id=1, source_target_pairs={{0,8},{8,0},{16,24},{24,16},{1,9},{9,1},{17,25},{25,17},{2,10},{10... | collective-permute-start | bytes 5308424 | tf_op jit(solution)/shard_map/ppermute | solution.py:44
  760.2 24.8 %collective-permute-start.38 = (bf16[96,768]{1,0:T(8,128)(2,1)S(1)}, bf16[96,768]{1,0:T(8,128)(2,1)S(1)}, u32[]{:S(2)}, u32[]{:S(2)}) collective-permute-start(bf16[96,768]{1,0:T(8,128)(2,1)S(1)} %fusion.119), channel_id=1, source_target_pairs={{0,4},{1,5},{2,6},{3,7},{4,0},{5,1},{6,2},{7,3},{8,12},{9,13},{10,... | collective-permute-start | bytes 442376 | tf_op jit(solution)/shard_map/ppermute | solution.py:44
  763.4 19.7 %collective-permute-start.20 = (bf16[2,2,2,24,2304]{4,3,1,2,0:T(8,128)(2,1)S(1)}, bf16[2,2,2,24,2304]{4,3,1,2,0:T(8,128)(2,1)S(1)}, u32[]{:S(2)}, u32[]{:S(2)}) collective-permute-start(bf16[2,2,2,24,2304]{4,3,1,2,0:T(8,128)(2,1)S(1)} %fusion.98), channel_id=1, source_target_pairs={{0,1},{1,0},{2,3},{3,2},{4,5},{5,4},{6,7},{7,6},{8,9},{9,8},{10,11... | collective-permute-start | bytes 2654216 | tf_op jit(solution)/shard_map/ppermute | solution.py:44
  767.8 18.6 %collective-permute-start.33 = (bf16[24,3072]{1,0:T(8,128)(2,1)S(1)}, bf16[24,3072]{1,0:T(8,128)(2,1)S(1)}, u32[]{:S(2)}, u32[]{:S(2)}) collective-permute-start(bf16[24,3072]{1,0:T(8,128)(2,1)S(1)} %fusion.118), channel_id=1, source_target_pairs={{0,4},{1,5},{2,6},{3,7},{4,0},{5,1},{6,2},{7,3},{8,12},{9,13},{10,... | collective-permute-start | bytes 442376 | tf_op jit(solution)/shard_map/ppermute | solution.py:44
  (175 other events, 1789.8 us)
